TPU v7x, 512 devices: a whole 4x8x8 slice. The times are simulated.
512 devices in a mesh: tensor: 4 (over z_lo, core), context: 128 (over z_hi, x, y).
Axes of the slice: x: 4, y: 8, z: 8 (z_hi: 4, z_lo: 2; z = z_hi * 2 + z_lo), core: 2. Of those that a mesh axis runs over, the one named last changes fastest.
Arguments:
- inputs: bfloat16 [16384, 1024], P('context', 'tensor'), may hold values from -6 to 6
- gates: bfloat16 [16384, 1024], P('context', 'tensor'), may hold values from -6 to 6
- filters: float32 [16384, 256], P('context'), may hold values from -6 to 6
- skip: float32 [1024], P('tensor'), may hold values from 0.5 to 2
- out_grad: bfloat16 [16384, 1024], P('context', 'tensor'), may hold values from -6 to 6
Outputs:
- input_grad: bfloat16 [16384, 1024], P('context', 'tensor')
- gate_grad: bfloat16 [16384, 1024], P('context', 'tensor')
- filter_grad: float32 [16384, 256], P('context')
All inputs are finite; a program needn't handle non-finite values.
Results may differ from a plain program's by a relative error of at most 0.0015.
Values sent between devices are 32-bit elements; how exact they have to be, the bound alone decides.
No kernel may reach another device: no remote copies, remote signals or barrier semaphores. Data moves between devices by JAX's collectives and lax.ppermute only.
A program may use at most 64 MiB of HBM per device.

v0:
```python
import math

import jax
import jax.numpy as jnp
import numpy as np
from jax import lax
from jax.experimental import pallas as pl
from jax.experimental.pallas import tpu as pltpu
from jax.sharding import PartitionSpec as P

N = 128
F32 = jnp.float32
BF16 = jnp.bfloat16


def tables():
    length = N * N
    index = np.arange(N)
    turn = (np.outer(4 * index + 1, index) % (4 * N)) * (2 * math.pi / (4 * N))
    first = [np.cos(turn), -np.sin(turn)]
    scale = 1.0 / (length * math.sqrt(length))
    last = [first[0].T * scale, first[1].T * scale]
    turn = np.outer(4 * index + 1, index) * (2 * math.pi / (4 * length))
    twist = [np.cos(turn), -np.sin(turn)]
    turn = (np.outer(index, index) % N) * (2 * math.pi / N)
    row = [np.cos(turn), -np.sin(turn)]
    return np.stack(first + twist + row + last).astype(np.float32)


def halves(value):
    high = value.astype(BF16)
    return high, (value - high.astype(F32)).astype(BF16)


def dot(a, b):
    return jnp.dot(a, b, preferred_element_type=F32)


def exact_dot(a, b):
    a_high, a_low = halves(a)
    b_high, b_low = halves(b)
    return dot(a_high, b_high) + (dot(a_low, b_high) + dot(a_high, b_low))


def pack_kernel(x_ref, g_ref, f_ref, o_ref, out_ref):
    x = x_ref[...].astype(F32)
    mixed = o_ref[...].astype(F32) * g_ref[...].astype(F32)
    for a, value in enumerate((x, mixed, f_ref[...])):
        for c in range(2):
            out_ref[pl.ds(2 * a + c, N, stride=6), :] = value[:, c * N : (c + 1) * N].T


def conv_kernel(in_ref, table_ref, out_ref):
    first = jnp.concatenate([table_ref[0], table_ref[1]], axis=0)
    tr, ti = table_ref[2], table_ref[3]
    rr, ri = table_ref[4], table_ref[5]
    forth = jnp.concatenate(
        [jnp.concatenate([rr, ri], axis=1), jnp.concatenate([-ri, rr], axis=1)], axis=0
    )
    back_table = jnp.concatenate(
        [jnp.concatenate([rr, -ri], axis=1), jnp.concatenate([ri, rr], axis=1)], axis=0
    )
    last = jnp.concatenate([table_ref[6], table_ref[7]], axis=1)
    field = jnp.concatenate([in_ref[pl.ds(s, N, stride=6), :] for s in range(6)], axis=1)
    spec = exact_dot(first, field)
    rows = []
    for s in range(6):
        re, im = spec[:N, s * N : (s + 1) * N], spec[N:, s * N : (s + 1) * N]
        rows.append(jnp.concatenate([re * tr - im * ti, re * ti + im * tr], axis=1))
    spec = exact_dot(jnp.concatenate(rows, axis=0), forth)

    def part(s):
        block = spec[s * N : (s + 1) * N]
        return block[:, :N], block[:, N:]

    conv, back, share = [], [], []
    for c in range(2):
        xr, xi = part(c)
        mr, mi = part(2 + c)
        fr, fi = part(4 + c)
        conv.append(jnp.concatenate([fr * xr - fi * xi, fr * xi + fi * xr], axis=1))
        back.append(jnp.concatenate([fr * mr + fi * mi, fr * mi - fi * mr], axis=1))
        share.append(jnp.concatenate([mr * xr + mi * xi, mi * xr - mr * xi], axis=1))
    spec = exact_dot(jnp.concatenate(conv + back + share, axis=0), back_table)
    columns = []
    for s in range(6):
        re, im = part(s)
        columns.append(jnp.concatenate([re * tr + im * ti, im * tr - re * ti], axis=0))
    result = exact_dot(last, jnp.concatenate(columns, axis=1))
    for s in range(6):
        out_ref[pl.ds(s, N, stride=6), :] = result[:, s * N : (s + 1) * N]


def share_kernel(in_ref, out_ref):
    for c in range(2):
        out_ref[:, c * N : (c + 1) * N] = in_ref[pl.ds(4 + c, N, stride=6), :].T


def unpack_kernel(in_ref, x_ref, g_ref, o_ref, skip_ref, input_ref, gate_ref):
    for c in range(2):
        at = slice(c * N, (c + 1) * N)
        x = x_ref[:, at].astype(F32)
        upstream = o_ref[:, at].astype(F32)
        mixed = upstream * g_ref[:, at].astype(F32)
        skip = skip_ref[:, at]
        conv = in_ref[pl.ds(c, N, stride=6), :].T
        back = in_ref[pl.ds(2 + c, N, stride=6), :].T
        input_ref[:, at] = (back + skip * mixed).astype(BF16)
        gate_ref[:, at] = (upstream * (conv + skip * x)).astype(BF16)


def call(kernel, out, *operands):
    return pl.pallas_call(
        kernel,
        out_shape=out,
        compiler_params=pltpu.CompilerParams(vmem_limit_bytes=24 << 20),
    )(*operands)


def shape(*dims, dtype=F32):
    return jax.ShapeDtypeStruct(dims, dtype)


def exchange(field):
    field = field.reshape(N, 1, 6 * N)
    field = lax.all_to_all(field, "context", split_axis=0, concat_axis=0, tiled=True)
    return field.reshape(6 * N, N)


def local(inputs, gates, filters, skip, out_grad):
    sent = call(pack_kernel, shape(6 * N, N), inputs, gates, filters, out_grad)
    taken = exchange(sent)
    sent = call(conv_kernel, shape(6 * N, N), taken, jnp.asarray(tables()))
    taken = exchange(sent)
    share = call(share_kernel, shape(N, 2 * N), taken)
    share = share + lax.ppermute(share, "tensor", [(i, i ^ 1) for i in range(4)])
    share = share + lax.ppermute(share, "tensor", [(i, i ^ 2) for i in range(4)])
    half = shape(N, 2 * N, dtype=BF16)
    input_grad, gate_grad = call(
        unpack_kernel, (half, half), taken, inputs, gates, out_grad, skip.reshape(1, 2 * N)
    )
    return input_grad, gate_grad, share


def solution(mesh):
    return jax.shard_map(
        local,
        mesh=mesh,
        in_specs=(
            P("context", "tensor"),
            P("context", "tensor"),
            P("context", None),
            P("tensor"),
            P("context", "tensor"),
        ),
        out_specs=(P("context", "tensor"), P("context", "tensor"), P("context", None)),
        check_vma=False,
    )
```

profile of v0, /device:TPU:1, one launch (start us, length us, event | category | flops | bytes accessed | tf_op | source)
XLA Modules:
  0.0 82.0 jit_solution(538785399959529330)
XLA Ops:
  0.6 0.0 copy-start.1
  0.6 0.8 %copy-done.1 = bf16[128,256]{1,0:T(8,128)(2,1)S(1)} copy-done((bf16[128,256]{1,0:T(8,128)(2,1)S(1)}, bf16[128,256]{1,0:T(8,128)(2,1)}, u32[]{:S(2)}) %copy-start.1) | copy-done | bytes 65560
  1.5 0.8 %copy-done.3 = bf16[128,256]{1,0:T(8,128)(2,1)S(1)} copy-done((bf16[128,256]{1,0:T(8,128)(2,1)S(1)}, bf16[128,256]{1,0:T(8,128)(2,1)}, u32[]{:S(2)}) %copy-start.3) | copy-done | bytes 65560
  2.3 0.8 %copy-done.5 = bf16[128,256]{1,0:T(8,128)(2,1)S(1)} copy-done((bf16[128,256]{1,0:T(8,128)(2,1)S(1)}, bf16[128,256]{1,0:T(8,128)(2,1)}, u32[]{:S(2)}) %copy-start.5) | copy-done | bytes 65560
  3.2 0.9 %copy-done.7 = f32[128,256]{1,0:T(8,128)S(1)} copy-done((f32[128,256]{1,0:T(8,128)S(1)}, f32[128,256]{1,0:T(8,128)}, u32[]{:S(2)}) %copy-start.7) | copy-done | bytes 131096
  4.1 0.2 shard_map.85
  4.2 0.0 copy-start
  4.2 38.1 %all_to_all.10 = f32[128,1,768]{2,1,0:T(1,128)S(1)} all-to-all(f32[128,1,768]{2,1,0:T(1,128)S(1)} %bitcast.9), channel_id=1, replica_groups=mesh['tensor'=4,'context'=128] {'context'}, dimensions={0} | all-to-all | bytes 786432 | tf_op jit(solution)/shard_map/all_to_all | solution.py:126
  42.4 0.0 copy-done
  42.4 2.3 %shard_map.86 = f32[768,128]{1,0:T(8,128)S(1)} custom-call(f32[768,128]{1,0:T(8,128)S(1)} %bitcast.7, f32[8,128,128]{2,1,0:T(8,128)S(1)} %copy-done), custom_call_target="tpu_custom_call" | custom-call | tf_op jit(solution)/shard_map/pallas_call | solution.py:113
  44.7 23.4 %all_to_all.11 = f32[128,1,768]{2,1,0:T(1,128)S(1)} all-to-all(f32[128,1,768]{2,1,0:T(1,128)S(1)} %bitcast.8), channel_id=1, replica_groups=mesh['tensor'=4,'context'=128] {'context'}, dimensions={0} | all-to-all | bytes 786432 | tf_op jit(solution)/shard_map/all_to_all | solution.py:126
  68.1 0.1 shard_map.88
  68.2 0.0 copy-start.2
  68.2 0.0 copy-start.4
  68.2 0.0 copy-start.6
  68.3 5.5 %collective-permute-start = (f32[128,256]{1,0:T(8,128)S(1)}, f32[128,256]{1,0:T(8,128)S(1)}, u32[]{:S(2)}, u32[]{:S(2)}) collective-permute-start(f32[128,256]{1,0:T(8,128)S(1)} %shard_map.88), channel_id=1, source_target_pairs={{0,128},{128,0},{256,384},{384,256},{1,129},{129,1},{257,385},{385... | collective-permute-start | bytes 393224 | tf_op jit(solution)/shard_map/ppermute | solution.py:136
  73.7 1.0 %collective-permute-done = f32[128,256]{1,0:T(8,128)S(1)} collective-permute-done((f32[128,256]{1,0:T(8,128)S(1)}, f32[128,256]{1,0:T(8,128)S(1)}, u32[]{:S(2)}, u32[]{:S(2)}) %collective-permute-start) | collective-permute-done | bytes 131104 | tf_op jit(solution)/shard_map/ppermute | solution.py:136
  74.7 0.0 copy-start.8
  74.7 3.1 %collective-permute-start.1 = (f32[128,256]{1,0:T(8,128)S(1)}, f32[128,256]{1,0:T(8,128)S(1)}, u32[]{:S(2)}, u32[]{:S(2)}) collective-permute-start(f32[128,256]{1,0:T(8,128)S(1)} %add.6), channel_id=1, source_target_pairs={{0,256},{128,384},{256,0},{384,128},{1,257},{129,385},{257,1},{385... | collective-permute-start | bytes 393224 | tf_op jit(solution)/shard_map/ppermute | solution.py:137
  77.8 0.0 copy-done.2
  77.9 0.0 copy-done.4
  77.9 0.8 shard_map.87
  78.7 2.7 %collective-permute-done.1 = f32[128,256]{1,0:T(8,128)S(1)} collective-permute-done((f32[128,256]{1,0:T(8,128)S(1)}, f32[128,256]{1,0:T(8,128)S(1)}, u32[]{:S(2)}, u32[]{:S(2)}) %collective-permute-start.1) | collective-permute-done | bytes 131104 | tf_op jit(solution)/shard_map/ppermute | solution.py:137
  81.4 0.7 add.7
  (6 shorter events, 0.0 us)
Async XLA Ops:
  0.6 0.8 %copy-start.1 = (bf16[128,256]{1,0:T(8,128)(2,1)S(1)}, bf16[128,256]{1,0:T(8,128)(2,1)}, u32[]{:S(2)}) copy-start(bf16[128,256]{1,0:T(8,128)(2,1)} %x_ref.3) | copy-start | bytes 196612
  1.5 0.8 %copy-start.3 = (bf16[128,256]{1,0:T(8,128)(2,1)S(1)}, bf16[128,256]{1,0:T(8,128)(2,1)}, u32[]{:S(2)}) copy-start(bf16[128,256]{1,0:T(8,128)(2,1)} %g_ref.3) | copy-start | bytes 196612
  2.3 0.8 %copy-start.5 = (bf16[128,256]{1,0:T(8,128)(2,1)S(1)}, bf16[128,256]{1,0:T(8,128)(2,1)}, u32[]{:S(2)}) copy-start(bf16[128,256]{1,0:T(8,128)(2,1)} %o_ref.3) | copy-start | bytes 196612
  3.2 0.9 %copy-start.7 = (f32[128,256]{1,0:T(8,128)S(1)}, f32[128,256]{1,0:T(8,128)}, u32[]{:S(2)}) copy-start(f32[128,256]{1,0:T(8,128)} %f_ref.1) | copy-start | bytes 393220
  4.2 38.2 %copy-start = (f32[8,128,128]{2,1,0:T(8,128)S(1)}, f32[8,128,128]{2,1,0:T(8,128)}, u32[]{:S(2)}) copy-start(f32[8,128,128]{2,1,0:T(8,128)} %constant.2.clone.table_ref) | copy-start | bytes 1572868
  68.2 9.6 %copy-start.2 = (bf16[128,256]{1,0:T(8,128)(2,1)S(1)}, bf16[128,256]{1,0:T(8,128)(2,1)}, u32[]{:S(2)}) copy-start(bf16[128,256]{1,0:T(8,128)(2,1)} %x_ref.3) | copy-start | bytes 196612
  68.2 9.6 %copy-start.4 = (bf16[128,256]{1,0:T(8,128)(2,1)S(1)}, bf16[128,256]{1,0:T(8,128)(2,1)}, u32[]{:S(2)}) copy-start(bf16[128,256]{1,0:T(8,128)(2,1)} %g_ref.3) | copy-start | bytes 196612
  68.2 9.6 %copy-start.6 = (bf16[128,256]{1,0:T(8,128)(2,1)S(1)}, bf16[128,256]{1,0:T(8,128)(2,1)}, u32[]{:S(2)}) copy-start(bf16[128,256]{1,0:T(8,128)(2,1)} %o_ref.3) | copy-start | bytes 196612
  68.3 6.5 %collective-permute-start = (f32[128,256]{1,0:T(8,128)S(1)}, f32[128,256]{1,0:T(8,128)S(1)}, u32[]{:S(2)}, u32[]{:S(2)}) collective-permute-start(f32[128,256]{1,0:T(8,128)S(1)} %shard_map.88), channel_id=1, source_target_pairs={{0,128},{128,0},{256,384},{384,256},{1,129},{129,1},{257,385},{385... | collective-permute-start | bytes 393224 | tf_op jit(solution)/shard_map/ppermute | solution.py:136
  74.7 3.2 %copy-start.8 = (f32[256]{0:T(256)S(1)}, f32[256]{0:T(256)}, u32[]{:S(2)}) copy-start(f32[256]{0:T(256)} %param.9) | copy-start | bytes 3076
  74.7 6.6 %collective-permute-start.1 = (f32[128,256]{1,0:T(8,128)S(1)}, f32[128,256]{1,0:T(8,128)S(1)}, u32[]{:S(2)}, u32[]{:S(2)}) collective-permute-start(f32[128,256]{1,0:T(8,128)S(1)} %add.6), channel_id=1, source_target_pairs={{0,256},{128,384},{256,0},{384,128},{1,257},{129,385},{257,1},{385... | collective-permute-start | bytes 393224 | tf_op jit(solution)/shard_map/ppermute | solution.py:137
where the time goes:
time: 82.5 us; the launch traced here: 82 us
  blocking collectives  61.6 us (75%)
  starting transfers between devices  8.58 us (10%)
  waiting for transfers between devices  3.64 us (4%)
  local copies, waits for them, and re-layouts  3.45 us (4%)
  Pallas kernels  3.35 us (4%)
    all_to_all x2, blocking collectives, exchange(): lax.all_to_all(field, 'context', split_axis=0, concat_axis=0, tiled=True)  61.6 us
    ppermute x1, starting transfers between devices, local(): lax.ppermute(share, 'tensor', [(i, i ^ 1) for i in range(4)])  5.48 us
    unnamed x18, local copies, waits for them, and re-layouts  3.45 us
    pallas_call x4, Pallas kernels, call(): pl.pallas_call(kernel, out_shape=out, compiler_params=pltpu.CompilerParam...  3.35 us
    ppermute x1, starting transfers between devices, local(): lax.ppermute(share, 'tensor', [(i, i ^ 2) for i in range(4)])  3.1 us
    ppermute x1, waiting for transfers between devices, local(): lax.ppermute(share, 'tensor', [(i, i ^ 2) for i in range(4)])  2.68 us
  transfers between devices with their start and end apart: 2, of which 2 were waited for; matrix products, arithmetic and copies ran while one was open for 0% of the time, Pallas kernels for 1%

commit v1 on v0

v1 whole, which is shorter than its diff:
```python
import functools
import math

import jax
import jax.numpy as jnp
import numpy as np
from jax import lax
from jax.experimental import pallas as pl
from jax.experimental.pallas import tpu as pltpu
from jax.sharding import PartitionSpec as P

N = 128
S = 5
F32 = jnp.float32
BF16 = jnp.bfloat16
HBM = pl.BlockSpec(memory_space=pltpu.HBM)


def tables():
    length = N * N
    index = np.arange(N)
    turn = (np.outer(4 * index + 1, index) % (4 * N)) * (2 * math.pi / (4 * N))
    first = [np.cos(turn), -np.sin(turn)]
    scale = 1.0 / (length * math.sqrt(length))
    last = [first[0].T * scale, first[1].T * scale]
    turn = np.outer(4 * index + 1, index) * (2 * math.pi / (4 * length))
    twist = [np.cos(turn), -np.sin(turn)]
    turn = (np.outer(index, index) % N) * (2 * math.pi / N)
    row = [np.cos(turn), -np.sin(turn)]
    return np.stack(first + twist + row + last).astype(np.float32)


def halves(value):
    high = value.astype(BF16)
    return high, (value - high.astype(F32)).astype(BF16)


def dot(a, b):
    return jnp.dot(a, b, preferred_element_type=F32)


def exact_dot(a, b):
    a_high, a_low = halves(a)
    b_high, b_low = halves(b)
    return dot(a_high, b_high) + (dot(a_low, b_high) + dot(a_high, b_low))


def across(*blocks):
    return jnp.concatenate(blocks, axis=1)


def down(*blocks):
    return jnp.concatenate(blocks, axis=0)


def forward(signals, table):
    spec = exact_dot(down(table[0], table[1]), across(*signals))
    tr, ti = table[2], table[3]
    rows = []
    for s in range(len(signals)):
        re, im = spec[:N, s * N : (s + 1) * N], spec[N:, s * N : (s + 1) * N]
        rows.append(across(re * tr - im * ti, re * ti + im * tr))
    rr, ri = table[4], table[5]
    spec = exact_dot(down(*rows), down(across(rr, ri), across(-ri, rr)))
    return [spec[s * N : (s + 1) * N] for s in range(len(signals))]


def inverse(spectra, table):
    rr, ri = table[4], table[5]
    spec = exact_dot(down(*spectra), down(across(rr, -ri), across(ri, rr)))
    tr, ti = table[2], table[3]
    columns = []
    for s in range(len(spectra)):
        re, im = spec[s * N : (s + 1) * N, :N], spec[s * N : (s + 1) * N, N:]
        columns.append(down(re * tr + im * ti, im * tr - re * ti))
    result = exact_dot(across(table[6], table[7]), across(*columns))
    return [result[:, s * N : (s + 1) * N] for s in range(len(spectra))]


def times(a, b):
    ar, ai, br, bi = a[:, :N], a[:, N:], b[:, :N], b[:, N:]
    return across(ar * br - ai * bi, ar * bi + ai * br)


def times_conj(a, b):
    ar, ai, br, bi = a[:, :N], a[:, N:], b[:, :N], b[:, N:]
    return across(ar * br + ai * bi, ai * br - ar * bi)


def core_index():
    return lax.axis_index("tensor") % 2


def signal_rows(ref, s):
    return ref.at[pl.ds(s, N, stride=S), :]


def pack_kernel(
    x_hbm, g_hbm, f_hbm, o_hbm, skip_hbm, out_ref, skip_ref, x_ref, g_ref, f_ref, o_ref, sems
):
    at = pl.multiple_of(core_index() * N, N)
    copies = [
        pltpu.make_async_copy(src, dst, sems.at[i])
        for i, (src, dst) in enumerate(
            [
                (x_hbm, x_ref),
                (f_hbm.at[:, pl.ds(at, N)], f_ref),
                (g_hbm, g_ref),
                (o_hbm, o_ref),
                (skip_hbm, skip_ref),
            ]
        )
    ]
    for copy in copies:
        copy.start()
    copies[0].wait()
    x = x_ref[...].astype(F32)
    for c in range(2):
        signal_rows(out_ref, c)[...] = x[:, c * N : (c + 1) * N].T
    copies[1].wait()
    signal_rows(out_ref, 4)[...] = f_ref[...].T
    copies[2].wait()
    copies[3].wait()
    mixed = o_ref[...].astype(F32) * g_ref[...].astype(F32)
    for c in range(2):
        signal_rows(out_ref, 2 + c)[...] = mixed[:, c * N : (c + 1) * N].T
    copies[4].wait()


def share_kernel(in_ref, table_ref, spec_ref, own_ref, out_ref):
    table = [table_ref[i] for i in range(8)]
    x0, x1, m0, m1 = forward([signal_rows(in_ref, s)[...] for s in range(4)], table)
    for s, spec in enumerate((x0, x1, m0, m1)):
        spec_ref[s] = spec
    share = inverse([times_conj(m0, x0), times_conj(m1, x1)], table)
    first = core_index() == 0
    own_ref[...] = jnp.where(first, share[0], share[1])
    out_ref[:N] = signal_rows(in_ref, 4)[...]
    out_ref[N:] = jnp.where(first, share[1], share[0])


def conv_kernel(spec_ref, own_ref, pair_ref, table_ref, out_ref):
    table = [table_ref[i] for i in range(8)]
    f0, f1 = forward([pair_ref[0, :N], pair_ref[1, :N]], table)
    x0, x1, m0, m1 = (spec_ref[s] for s in range(4))
    results = inverse(
        [times(f0, x0), times(f1, x1), times_conj(m0, f0), times_conj(m1, f1)], table
    )
    for s, result in enumerate(results):
        signal_rows(out_ref, s)[...] = result
    signal_rows(out_ref, 4)[...] = own_ref[...] + pair_ref[1 - core_index(), N:]


def shared_kernel(in_ref, out_ref):
    out_ref[...] = signal_rows(in_ref, 4)[...].T


def unpack_kernel(
    in_ref, all_ref, x_ref, g_ref, o_ref, skip_ref, input_ref, gate_ref, share_ref
):
    for c in range(2):
        at = slice(c * N, (c + 1) * N)
        share_ref[:, at] = all_ref[c] + all_ref[2 + c]
        x = x_ref[:, at].astype(F32)
        upstream = o_ref[:, at].astype(F32)
        mixed = upstream * g_ref[:, at].astype(F32)
        skip = skip_ref[:, at]
        conv = signal_rows(in_ref, c)[...].T
        back = signal_rows(in_ref, 2 + c)[...].T
        input_ref[:, at] = (back + skip * mixed).astype(BF16)
        gate_ref[:, at] = (upstream * (conv + skip * x)).astype(BF16)


def shape(*dims, dtype=F32):
    return jax.ShapeDtypeStruct(dims, dtype)


def call(kernel, out, *operands, **options):
    return pl.pallas_call(
        kernel,
        out_shape=out,
        compiler_params=pltpu.CompilerParams(vmem_limit_bytes=16 << 20),
        **options,
    )(*operands)


def exchange(field):
    field = field.reshape(N, 1, S * N)
    field = lax.all_to_all(field, "context", split_axis=0, concat_axis=0, tiled=True)
    return field.reshape(S * N, N)


def core_groups(size):
    return [[i, i + 1] for i in range(0, size, 2)]


def local(inputs, gates, filters, skip, out_grad):
    tensor = lax.axis_size("tensor")
    table = jnp.asarray(tables())
    sent, skip = call(
        pack_kernel,
        (pltpu.VMEM((S * N, N), F32), pltpu.VMEM((1, 2 * N), F32)),
        *(
            pltpu.with_memory_space_constraint(operand, pltpu.HBM)
            for operand in (inputs, gates, filters, out_grad, skip.reshape(1, 2 * N))
        ),
        in_specs=[HBM] * 5,
        scratch_shapes=[
            pltpu.VMEM((N, 2 * N), BF16),
            pltpu.VMEM((N, 2 * N), BF16),
            pltpu.VMEM((N, N), F32),
            pltpu.VMEM((N, 2 * N), BF16),
            pltpu.SemaphoreType.DMA((5,)),
        ],
    )
    taken = exchange(sent)
    spec, own, pair = call(
        share_kernel, (shape(4, N, 2 * N), shape(N, N), shape(2 * N, N)), taken, table
    )
    pair = lax.all_gather(
        pair, "tensor", axis=0, tiled=False, axis_index_groups=core_groups(tensor)
    )
    sent = call(conv_kernel, shape(S * N, N), spec, own, pair, table)
    taken = exchange(sent)
    share = call(shared_kernel, pltpu.VMEM((N, N), F32), taken)
    share = lax.all_gather(share, "tensor", axis=0, tiled=False)
    half = shape(N, 2 * N, dtype=BF16)
    return call(
        unpack_kernel,
        (half, half, shape(N, 2 * N)),
        taken,
        pltpu.with_memory_space_constraint(share, pltpu.VMEM),
        inputs,
        gates,
        out_grad,
        skip,
    )


def solution(mesh):
    return jax.shard_map(
        local,
        mesh=mesh,
        in_specs=(
            P("context", "tensor"),
            P("context", "tensor"),
            P("context", None),
            P("tensor"),
            P("context", "tensor"),
        ),
        out_specs=(P("context", "tensor"), P("context", "tensor"), P("context", None)),
        check_vma=False,
    )
```

time: 82.5 us -> 76.7 us (0.930)
  blocking collectives: 61.6 us -> 70.9 us
  starting transfers between devices: 8.58 us -> 0 us
  waiting for transfers between devices: 3.64 us -> 0 us
  local copies, waits for them, and re-layouts: 3.45 us -> 0.03 us
  Pallas kernels: 3.35 us -> 4.84 us
    all_gather x0 -> x2, blocking collectives: none -> 11.8 us  [the longest x1 7.6 us: local(): share = lax.all_gather(share, 'tensor', axis=0, tiled=False)]
    ppermute x2 -> x0, starting transfers between devices: 8.58 us -> none  [the longest x1 5.48 us: local(): lax.ppermute(share, 'tensor', [(i, i ^ 1) for i in range(4)])]
    ppermute x2 -> x0, waiting for transfers between devices: 3.64 us -> none  [the longest x1 2.68 us: local(): lax.ppermute(share, 'tensor', [(i, i ^ 2) for i in range(4)])]
    unnamed x18 -> x8, local copies, waits for them, and re-layouts: 3.45 us -> 0.03 us
    all_to_all x2, blocking collectives: 61.6 us -> 59.1 us  [exchange(): lax.all_to_all(field, 'context', split_axis=0, concat_axis=0, tiled=True)]
    pallas_call x4 -> x5, Pallas kernels: 3.35 us -> 4.84 us  [call(): pl.pallas_call(kernel, out_shape=out, compiler_params=pltpu.CompilerParam...]
  transfers between devices with their start and end apart: 2 -> 0, of which waited for: 2 -> 0; matrix products, arithmetic and copies ran while one was open for 0% -> 0% of each run, Pallas kernels for 1% -> 0%
where the time goes in v1:
time: 76.7 us; the launch traced here: 76.4 us
  blocking collectives  70.9 us (92%)
  Pallas kernels  4.84 us (6%)
    all_to_all x2, blocking collectives, exchange(): lax.all_to_all(field, 'context', split_axis=0, concat_axis=0, tiled=True)  59.1 us
    all_gather x1, blocking collectives, local(): share = lax.all_gather(share, 'tensor', axis=0, tiled=False)  7.6 us
    pallas_call x5, Pallas kernels, call(): pl.pallas_call(kernel, out_shape=out, compiler_params=pltpu.CompilerParam...  4.84 us
    all_gather x1, blocking collectives, local(): lax.all_gather(pair, 'tensor', axis=0, tiled=False, axis_index_groups=cor...  4.19 us

profile of v1, /device:TPU:1, one launch (start us, length us, event | category | flops | bytes accessed | tf_op | source)
XLA Modules:
  0.0 76.4 jit_solution(8931096917230496669)
XLA Ops:
  0.6 0.0 copy-start
  0.6 1.3 %shard_map.85 = (f32[640,128]{1,0:T(8,128)S(1)}, f32[1,256]{1,0:T(1,128)S(1)}) custom-call(bf16[128,256]{1,0:T(8,128)(2,1)} %x_ref.1, bf16[128,256]{1,0:T(8,128)(2,1)} %g_ref.1, f32[128,256]{1,0:T(8,128)} %f_hbm.1, bf16[128,256]{1,0:T(8,128)(2,1)} %o_ref.1, f32[1,256]{1,0:T(1,128)} %bitcast.14), custom_call_target="tpu_custom_call" | custom-call | tf_op jit(solution)/shard_map/pallas_call | solution.py:179
  1.9 36.4 %all_to_all.10 = f32[128,1,640]{2,1,0:T(1,128)S(1)} all-to-all(f32[128,1,640]{2,1,0:T(1,128)S(1)} %bitcast.13), channel_id=1, replica_groups=mesh['tensor'=4,'context'=128] {'context'}, dimensions={0} | all-to-all | bytes 655360 | tf_op jit(solution)/shard_map/all_to_all | solution.py:189
  38.3 0.0 copy-done
  38.3 1.3 %shard_map.86 = (f32[4,128,256]{2,1,0:T(8,128)S(1)}, f32[128,128]{1,0:T(8,128)S(1)}, f32[256,128]{1,0:T(8,128)S(1)}) custom-call(f32[640,128]{1,0:T(8,128)S(1)} %bitcast.9, f32[8,128,128]{2,1,0:T(8,128)S(1)} %copy-done), custom_call_target="tpu_custom_call" | custom-call | tf_op jit(solution)/shard_map/pallas_call | solution.py:179
  39.6 4.2 %all-gather = f32[512,128]{1,0:T(8,128)S(1)} all-gather(f32[256,128]{1,0:T(8,128)S(1)} %get-tuple-element.11), channel_id=2, replica_groups={{0,128},{256,384},{1,129},{257,385},{2,130},{258,386},{3,131},{259,387}..., dimensions={0}, use_global_device_ids=true | all-gather | bytes 393216 | tf_op jit(solution)/shard_map/all_gather | solution.py:220
  43.8 1.3 %shard_map.87 = f32[640,128]{1,0:T(8,128)S(1)} custom-call(f32[4,128,256]{2,1,0:T(8,128)S(1)} %get-tuple-element.9.spec_ref, f32[128,128]{1,0:T(8,128)S(1)} %get-tuple-element.10.own_ref, f32[2,256,128]{2,1,0:T(8,128)S(1)} %bitcast.12, f32[8,128,128]{2,1,0:T(8,128)S(1)} %copy-done), custom_call_target="tpu_custom_call" | custom-call | tf_op jit(solution)/shard_map/pallas_call | solution.py:179
  45.1 22.7 %all_to_all.11 = f32[128,1,640]{2,1,0:T(1,128)S(1)} all-to-all(f32[128,1,640]{2,1,0:T(1,128)S(1)} %bitcast.10), channel_id=1, replica_groups=mesh['tensor'=4,'context'=128] {'context'}, dimensions={0} | all-to-all | bytes 655360 | tf_op jit(solution)/shard_map/all_to_all | solution.py:189
  67.9 0.1 shard_map.88
  67.9 0.0 copy-start.1
  68.0 0.0 copy-start.2
  68.0 0.0 copy-start.3
  68.0 7.6 %all-gather.1 = f32[512,128]{1,0:T(8,128)S(1)} all-gather(f32[128,128]{1,0:T(8,128)S(1)} %shard_map.88), channel_id=3, replica_groups=mesh['tensor'=4,'context'=128] {'tensor'}, dimensions={0}, use_global_device_ids=true | all-gather | bytes 327680 | tf_op jit(solution)/shard_map/all_gather | solution.py:226
  75.6 0.0 copy-done.1
  75.6 0.0 copy-done.2
  75.6 0.0 copy-done.3
  75.6 0.8 %shard_map.89 = (bf16[128,256]{1,0:T(8,128)(2,1)}, bf16[128,256]{1,0:T(8,128)(2,1)}, f32[128,256]{1,0:T(8,128)}) custom-call(f32[640,128]{1,0:T(8,128)S(1)} %bitcast.8, f32[4,128,128]{2,1,0:T(8,128)S(1)} %bitcast.11, bf16[128,256]{1,0:T(8,128)(2,1)S(1)} %copy-done.1, bf16[128,256]{1,0:T(8,128)(2,1)S(1)} %copy-done.2, bf16[128,256]{1,0:T(8,128)(2,1)S(1)} %copy-done.3, ...), custom_call_target="tpu_custom_call" | custom-call | tf_op jit(solution)/shard_map/pallas_call | solution.py:179
Async XLA Ops:
  0.6 37.7 %copy-start = (f32[8,128,128]{2,1,0:T(8,128)S(1)}, f32[8,128,128]{2,1,0:T(8,128)}, u32[]{:S(2)}) copy-start(f32[8,128,128]{2,1,0:T(8,128)} %constant.2.clone.table_ref) | copy-start | bytes 1572868
  67.9 7.6 %copy-start.1 = (bf16[128,256]{1,0:T(8,128)(2,1)S(1)}, bf16[128,256]{1,0:T(8,128)(2,1)}, u32[]{:S(2)}) copy-start(bf16[128,256]{1,0:T(8,128)(2,1)} %x_ref.1) | copy-start | bytes 196612
  68.0 7.6 %copy-start.2 = (bf16[128,256]{1,0:T(8,128)(2,1)S(1)}, bf16[128,256]{1,0:T(8,128)(2,1)}, u32[]{:S(2)}) copy-start(bf16[128,256]{1,0:T(8,128)(2,1)} %g_ref.1) | copy-start | bytes 196612
  68.0 7.6 %copy-start.3 = (bf16[128,256]{1,0:T(8,128)(2,1)S(1)}, bf16[128,256]{1,0:T(8,128)(2,1)}, u32[]{:S(2)}) copy-start(bf16[128,256]{1,0:T(8,128)(2,1)} %o_ref.1) | copy-start | bytes 196612

commit v2 on v1

--- a/solution.py
+++ b/solution.py
@@ -42,7 +42,7 @@
 def exact_dot(a, b):
     a_high, a_low = halves(a)
     b_high, b_low = halves(b)
-    return dot(a_high, b_high) + (dot(a_low, b_high) + dot(a_high, b_low))
+    return dot(across(a_high, a_low, a_high), down(b_high, b_high, b_low))
 
 
 def across(*blocks):
@@ -129,26 +129,27 @@
 
 def share_kernel(in_ref, table_ref, spec_ref, own_ref, out_ref):
     table = [table_ref[i] for i in range(8)]
-    x0, x1, m0, m1 = forward([signal_rows(in_ref, s)[...] for s in range(4)], table)
+    x0, x1, m0, m1, f = forward([signal_rows(in_ref, s)[...] for s in range(S)], table)
     for s, spec in enumerate((x0, x1, m0, m1)):
         spec_ref[s] = spec
     share = inverse([times_conj(m0, x0), times_conj(m1, x1)], table)
     first = core_index() == 0
     own_ref[...] = jnp.where(first, share[0], share[1])
-    out_ref[:N] = signal_rows(in_ref, 4)[...]
-    out_ref[N:] = jnp.where(first, share[1], share[0])
+    out_ref[0] = f[:, :N]
+    out_ref[1] = f[:, N:]
+    out_ref[2] = jnp.where(first, share[1], share[0])
 
 
 def conv_kernel(spec_ref, own_ref, pair_ref, table_ref, out_ref):
     table = [table_ref[i] for i in range(8)]
-    f0, f1 = forward([pair_ref[0, :N], pair_ref[1, :N]], table)
+    f0, f1 = (across(pair_ref[c, 0], pair_ref[c, 1]) for c in range(2))
     x0, x1, m0, m1 = (spec_ref[s] for s in range(4))
     results = inverse(
         [times(f0, x0), times(f1, x1), times_conj(m0, f0), times_conj(m1, f1)], table
     )
     for s, result in enumerate(results):
         signal_rows(out_ref, s)[...] = result
-    signal_rows(out_ref, 4)[...] = own_ref[...] + pair_ref[1 - core_index(), N:]
+    signal_rows(out_ref, 4)[...] = own_ref[...] + pair_ref[1 - core_index(), 2]
 
 
 def shared_kernel(in_ref, out_ref):
@@ -215,7 +216,7 @@
     )
     taken = exchange(sent)
     spec, own, pair = call(
-        share_kernel, (shape(4, N, 2 * N), shape(N, N), shape(2 * N, N)), taken, table
+        share_kernel, (shape(4, N, 2 * N), shape(N, N), shape(3, N, N)), taken, table
     )
     pair = lax.all_gather(
         pair, "tensor", axis=0, tiled=False, axis_index_groups=core_groups(tensor)

time: 76.7 us -> 76.2 us (level)
  no operation moved by 1% of the time
where the time goes in v2:
time: 76.2 us; the launch traced here: 76 us
  blocking collectives  70.9 us (93%)
  Pallas kernels  4.28 us (6%)
    all_to_all x2, blocking collectives, exchange(): lax.all_to_all(field, 'context', split_axis=0, concat_axis=0, tiled=True)  59.1 us
    all_gather x1, blocking collectives, local(): share = lax.all_gather(share, 'tensor', axis=0, tiled=False)  7.61 us
    pallas_call x5, Pallas kernels, call(): pl.pallas_call(kernel, out_shape=out, compiler_params=pltpu.CompilerParam...  4.28 us
    all_gather x1, blocking collectives, local(): lax.all_gather(pair, 'tensor', axis=0, tiled=False, axis_index_groups=cor...  4.28 us

profile of v2, /device:TPU:1, one launch (start us, length us, event | category | flops | bytes accessed | tf_op | source)
XLA Modules:
  0.0 76.0 jit_solution(921699089581614755)
XLA Ops:
  0.6 0.0 copy-start
  0.6 1.3 %shard_map.85 = (f32[640,128]{1,0:T(8,128)S(1)}, f32[1,256]{1,0:T(1,128)S(1)}) custom-call(bf16[128,256]{1,0:T(8,128)(2,1)} %x_ref.1, bf16[128,256]{1,0:T(8,128)(2,1)} %g_ref.1, f32[128,256]{1,0:T(8,128)} %f_hbm.1, bf16[128,256]{1,0:T(8,128)(2,1)} %o_ref.1, f32[1,256]{1,0:T(1,128)} %bitcast.14), custom_call_target="tpu_custom_call" | custom-call | tf_op jit(solution)/shard_map/pallas_call | solution.py:180
  1.9 36.4 %all_to_all.10 = f32[128,1,640]{2,1,0:T(1,128)S(1)} all-to-all(f32[128,1,640]{2,1,0:T(1,128)S(1)} %bitcast.13), channel_id=1, replica_groups=mesh['tensor'=4,'context'=128] {'context'}, dimensions={0} | all-to-all | bytes 655360 | tf_op jit(solution)/shard_map/all_to_all | solution.py:190
  38.3 0.0 copy-done
  38.3 1.3 %shard_map.86 = (f32[4,128,256]{2,1,0:T(8,128)S(1)}, f32[128,128]{1,0:T(8,128)S(1)}, f32[3,128,128]{2,1,0:T(8,128)S(1)}) custom-call(f32[640,128]{1,0:T(8,128)S(1)} %bitcast.11, f32[8,128,128]{2,1,0:T(8,128)S(1)} %copy-done), custom_call_target="tpu_custom_call" | custom-call | tf_op jit(solution)/shard_map/pallas_call | solution.py:180
  39.6 4.3 %all-gather = f32[6,128,128]{2,1,0:T(8,128)S(1)} all-gather(f32[3,128,128]{2,1,0:T(8,128)S(1)} %get-tuple-element.11), channel_id=2, replica_groups={{0,128},{256,384},{1,129},{257,385},{2,130},{258,386},{3,131},{259,387}..., dimensions={0}, use_global_device_ids=true | all-gather | bytes 589824 | tf_op jit(solution)/shard_map/all_gather | solution.py:221
  43.9 0.8 shard_map.87
  44.7 22.7 %all_to_all.11 = f32[128,1,640]{2,1,0:T(1,128)S(1)} all-to-all(f32[128,1,640]{2,1,0:T(1,128)S(1)} %bitcast.10), channel_id=1, replica_groups=mesh['tensor'=4,'context'=128] {'context'}, dimensions={0} | all-to-all | bytes 655360 | tf_op jit(solution)/shard_map/all_to_all | solution.py:190
  67.4 0.1 shard_map.88
  67.5 0.0 copy-start.1
  67.5 0.0 copy-start.2
  67.5 0.0 copy-start.3
  67.5 7.6 %all-gather.1 = f32[512,128]{1,0:T(8,128)S(1)} all-gather(f32[128,128]{1,0:T(8,128)S(1)} %shard_map.88), channel_id=3, replica_groups=mesh['tensor'=4,'context'=128] {'tensor'}, dimensions={0}, use_global_device_ids=true | all-gather | bytes 327680 | tf_op jit(solution)/shard_map/all_gather | solution.py:227
  75.1 0.0 copy-done.1
  75.1 0.0 copy-done.2
  75.1 0.0 copy-done.3
  75.1 0.8 %shard_map.89 = (bf16[128,256]{1,0:T(8,128)(2,1)}, bf16[128,256]{1,0:T(8,128)(2,1)}, f32[128,256]{1,0:T(8,128)}) custom-call(f32[640,128]{1,0:T(8,128)S(1)} %bitcast.8, f32[4,128,128]{2,1,0:T(8,128)S(1)} %bitcast.12, bf16[128,256]{1,0:T(8,128)(2,1)S(1)} %copy-done.1, bf16[128,256]{1,0:T(8,128)(2,1)S(1)} %copy-done.2, bf16[128,256]{1,0:T(8,128)(2,1)S(1)} %copy-done.3, ...), custom_call_target="tpu_custom_call" | custom-call | tf_op jit(solution)/shard_map/pallas_call | solution.py:180
Async XLA Ops:
  0.6 37.7 %copy-start = (f32[8,128,128]{2,1,0:T(8,128)S(1)}, f32[8,128,128]{2,1,0:T(8,128)}, u32[]{:S(2)}) copy-start(f32[8,128,128]{2,1,0:T(8,128)} %constant.2.clone.table_ref) | copy-start | bytes 1572868
  67.5 7.7 %copy-start.1 = (bf16[128,256]{1,0:T(8,128)(2,1)S(1)}, bf16[128,256]{1,0:T(8,128)(2,1)}, u32[]{:S(2)}) copy-start(bf16[128,256]{1,0:T(8,128)(2,1)} %x_ref.1) | copy-start | bytes 196612
  67.5 7.6 %copy-start.2 = (bf16[128,256]{1,0:T(8,128)(2,1)S(1)}, bf16[128,256]{1,0:T(8,128)(2,1)}, u32[]{:S(2)}) copy-start(bf16[128,256]{1,0:T(8,128)(2,1)} %g_ref.1) | copy-start | bytes 196612
  67.5 7.6 %copy-start.3 = (bf16[128,256]{1,0:T(8,128)(2,1)S(1)}, bf16[128,256]{1,0:T(8,128)(2,1)}, u32[]{:S(2)}) copy-start(bf16[128,256]{1,0:T(8,128)(2,1)} %o_ref.1) | copy-start | bytes 196612

commit v3 on v2

--- a/solution.py
+++ b/solution.py
@@ -16,10 +16,14 @@
 HBM = pl.BlockSpec(memory_space=pltpu.HBM)
 
 
+def partners():
+    return np.random.default_rng(16).permutation(N)
+
+
 def tables():
     length = N * N
     index = np.arange(N)
-    turn = (np.outer(4 * index + 1, index) % (4 * N)) * (2 * math.pi / (4 * N))
+    turn = (np.outer(4 * index + 1, partners()) % (4 * N)) * (2 * math.pi / (4 * N))
     first = [np.cos(turn), -np.sin(turn)]
     scale = 1.0 / (length * math.sqrt(length))
     last = [first[0].T * scale, first[1].T * scale]
@@ -103,10 +107,10 @@
         pltpu.make_async_copy(src, dst, sems.at[i])
         for i, (src, dst) in enumerate(
             [
+                (g_hbm, g_ref),
+                (o_hbm, o_ref),
                 (x_hbm, x_ref),
                 (f_hbm.at[:, pl.ds(at, N)], f_ref),
-                (g_hbm, g_ref),
-                (o_hbm, o_ref),
                 (skip_hbm, skip_ref),
             ]
         )
@@ -114,42 +118,41 @@
     for copy in copies:
         copy.start()
     copies[0].wait()
+    copies[1].wait()
+    mixed = o_ref[...].astype(F32) * g_ref[...].astype(F32)
+    for c in range(2):
+        signal_rows(out_ref, 2 + c)[...] = mixed[:, c * N : (c + 1) * N].T
+    copies[2].wait()
     x = x_ref[...].astype(F32)
     for c in range(2):
         signal_rows(out_ref, c)[...] = x[:, c * N : (c + 1) * N].T
-    copies[1].wait()
+    copies[3].wait()
     signal_rows(out_ref, 4)[...] = f_ref[...].T
-    copies[2].wait()
-    copies[3].wait()
-    mixed = o_ref[...].astype(F32) * g_ref[...].astype(F32)
-    for c in range(2):
-        signal_rows(out_ref, 2 + c)[...] = mixed[:, c * N : (c + 1) * N].T
     copies[4].wait()
 
 
-def share_kernel(in_ref, table_ref, spec_ref, own_ref, out_ref):
+def spectra_kernel(in_ref, table_ref, spec_ref, own_ref, out_ref):
     table = [table_ref[i] for i in range(8)]
     x0, x1, m0, m1, f = forward([signal_rows(in_ref, s)[...] for s in range(S)], table)
     for s, spec in enumerate((x0, x1, m0, m1)):
         spec_ref[s] = spec
-    share = inverse([times_conj(m0, x0), times_conj(m1, x1)], table)
+    share = times_conj(m0, x0), times_conj(m1, x1)
     first = core_index() == 0
     own_ref[...] = jnp.where(first, share[0], share[1])
-    out_ref[0] = f[:, :N]
-    out_ref[1] = f[:, N:]
-    out_ref[2] = jnp.where(first, share[1], share[0])
-
-
-def conv_kernel(spec_ref, own_ref, pair_ref, table_ref, out_ref):
+    out_ref[0] = f
+    out_ref[1] = jnp.where(first, share[1], share[0])
+
+
+def inverse_kernel(spec_ref, own_ref, pair_ref, table_ref, out_ref):
     table = [table_ref[i] for i in range(8)]
-    f0, f1 = (across(pair_ref[c, 0], pair_ref[c, 1]) for c in range(2))
+    f0, f1 = pair_ref[0, 0], pair_ref[1, 0]
     x0, x1, m0, m1 = (spec_ref[s] for s in range(4))
+    share = own_ref[...] + pair_ref[1 - core_index(), 1]
     results = inverse(
-        [times(f0, x0), times(f1, x1), times_conj(m0, f0), times_conj(m1, f1)], table
+        [times(f0, x0), times(f1, x1), times_conj(m0, f0), times_conj(m1, f1), share], table
     )
     for s, result in enumerate(results):
         signal_rows(out_ref, s)[...] = result
-    signal_rows(out_ref, 4)[...] = own_ref[...] + pair_ref[1 - core_index(), 2]
 
 
 def shared_kernel(in_ref, out_ref):
@@ -157,19 +160,42 @@
 
 
 def unpack_kernel(
-    in_ref, all_ref, x_ref, g_ref, o_ref, skip_ref, input_ref, gate_ref, share_ref
+    in_ref,
+    all_ref,
+    x_ref,
+    g_ref,
+    o_ref,
+    skip_ref,
+    input_hbm,
+    gate_hbm,
+    share_hbm,
+    input_ref,
+    gate_ref,
+    share_ref,
+    sems,
 ):
-    for c in range(2):
-        at = slice(c * N, (c + 1) * N)
+    copies = [
+        pltpu.make_async_copy(src, dst, sems.at[i])
+        for i, (src, dst) in enumerate(
+            [(share_ref, share_hbm), (input_ref, input_hbm), (gate_ref, gate_hbm)]
+        )
+    ]
+    halves_of = [slice(c * N, (c + 1) * N) for c in range(2)]
+    for c, at in enumerate(halves_of):
         share_ref[:, at] = all_ref[c] + all_ref[2 + c]
+    copies[0].start()
+    for c, at in enumerate(halves_of):
+        back = signal_rows(in_ref, 2 + c)[...].T
+        mixed = o_ref[:, at].astype(F32) * g_ref[:, at].astype(F32)
+        input_ref[:, at] = (back + skip_ref[:, at] * mixed).astype(BF16)
+    copies[1].start()
+    for c, at in enumerate(halves_of):
+        conv = signal_rows(in_ref, c)[...].T
         x = x_ref[:, at].astype(F32)
-        upstream = o_ref[:, at].astype(F32)
-        mixed = upstream * g_ref[:, at].astype(F32)
-        skip = skip_ref[:, at]
-        conv = signal_rows(in_ref, c)[...].T
-        back = signal_rows(in_ref, 2 + c)[...].T
-        input_ref[:, at] = (back + skip * mixed).astype(BF16)
-        gate_ref[:, at] = (upstream * (conv + skip * x)).astype(BF16)
+        gate_ref[:, at] = (o_ref[:, at].astype(F32) * (conv + skip_ref[:, at] * x)).astype(BF16)
+    copies[2].start()
+    for copy in copies:
+        copy.wait()
 
 
 def shape(*dims, dtype=F32):
@@ -187,7 +213,14 @@
 
 def exchange(field):
     field = field.reshape(N, 1, S * N)
-    field = lax.all_to_all(field, "context", split_axis=0, concat_axis=0, tiled=True)
+    field = lax.all_to_all(
+        field,
+        "context",
+        split_axis=0,
+        concat_axis=0,
+        tiled=True,
+        axis_index_groups=[partners().tolist()],
+    )
     return field.reshape(S * N, N)
 
 
@@ -216,12 +249,15 @@
     )
     taken = exchange(sent)
     spec, own, pair = call(
-        share_kernel, (shape(4, N, 2 * N), shape(N, N), shape(3, N, N)), taken, table
+        spectra_kernel,
+        (shape(4, N, 2 * N), shape(N, 2 * N), shape(2, N, 2 * N)),
+        taken,
+        table,
     )
     pair = lax.all_gather(
         pair, "tensor", axis=0, tiled=False, axis_index_groups=core_groups(tensor)
     )
-    sent = call(conv_kernel, shape(S * N, N), spec, own, pair, table)
+    sent = call(inverse_kernel, shape(S * N, N), spec, own, pair, table)
     taken = exchange(sent)
     share = call(shared_kernel, pltpu.VMEM((N, N), F32), taken)
     share = lax.all_gather(share, "tensor", axis=0, tiled=False)
@@ -235,6 +271,13 @@
         gates,
         out_grad,
         skip,
+        out_specs=(HBM,) * 3,
+        scratch_shapes=[
+            pltpu.VMEM((N, 2 * N), BF16),
+            pltpu.VMEM((N, 2 * N), BF16),
+            pltpu.VMEM((N, 2 * N), F32),
+            pltpu.SemaphoreType.DMA((3,)),
+        ],
     )
 
 

time: 76.2 us -> 71.5 us (0.938)
  blocking collectives: 70.9 us -> 66.7 us
    all_to_all x2, blocking collectives: 59.1 us -> 55.5 us  [exchange(): lax.all_to_all(field, 'context', split_axis=0, concat_axis=0, tiled=True,...]
where the time goes in v3:
time: 71.5 us; the launch traced here: 71.3 us
  blocking collectives  66.7 us (93%)
  Pallas kernels  3.82 us (5%)
    all_to_all x2, blocking collectives, exchange(): lax.all_to_all(field, 'context', split_axis=0, concat_axis=0, tiled=True,...  55.5 us
    all_gather x1, blocking collectives, local(): share = lax.all_gather(share, 'tensor', axis=0, tiled=False)  7.52 us
    pallas_call x5, Pallas kernels, call(): pl.pallas_call(kernel, out_shape=out, compiler_params=pltpu.CompilerParam...  3.82 us
    all_gather x1, blocking collectives, local(): lax.all_gather(pair, 'tensor', axis=0, tiled=False, axis_index_groups=cor...  3.68 us

profile of v3, /device:TPU:1, one launch (start us, length us, event | category | flops | bytes accessed | tf_op | source)
XLA Modules:
  0.0 71.3 jit_solution(3070361792762340094)
XLA Ops:
  0.6 0.0 copy-start
  0.6 1.3 %shard_map.85 = (f32[640,128]{1,0:T(8,128)S(1)}, f32[1,256]{1,0:T(1,128)S(1)}) custom-call(bf16[128,256]{1,0:T(8,128)(2,1)} %x_ref.1, bf16[128,256]{1,0:T(8,128)(2,1)} %g_ref.1, f32[128,256]{1,0:T(8,128)} %f_hbm.1, bf16[128,256]{1,0:T(8,128)(2,1)} %o_ref.1, f32[1,256]{1,0:T(1,128)} %bitcast.14), custom_call_target="tpu_custom_call" | custom-call | tf_op jit(solution)/shard_map/pallas_call | solution.py:206
  1.9 32.9 %all_to_all.10 = f32[128,1,640]{2,1,0:T(1,128)S(1)} all-to-all(f32[128,1,640]{2,1,0:T(1,128)S(1)} %bitcast.13), channel_id=1, replica_groups={{79,5,16,111,14,93,64,114,119,118,3,55,92,23,25,11,88,27,47,102,8,6,126..., dimensions={0} | all-to-all | bytes 655360 | tf_op jit(solution)/shard_map/all_to_all | solution.py:216
  34.9 0.0 copy-done
  34.9 0.7 %shard_map.86 = (f32[4,128,256]{2,1,0:T(8,128)S(1)}, f32[128,256]{1,0:T(8,128)S(1)}, f32[2,128,256]{2,1,0:T(8,128)S(1)}) custom-call(f32[640,128]{1,0:T(8,128)S(1)} %bitcast.11, f32[8,128,128]{2,1,0:T(8,128)S(1)} %copy-done), custom_call_target="tpu_custom_call" | custom-call | tf_op jit(solution)/shard_map/pallas_call | solution.py:206
  35.6 3.7 %all-gather = f32[4,128,256]{2,1,0:T(8,128)S(1)} all-gather(f32[2,128,256]{2,1,0:T(8,128)S(1)} %get-tuple-element.11), channel_id=2, replica_groups={{0,128},{256,384},{1,129},{257,385},{2,130},{258,386},{3,131},{259,387}..., dimensions={0}, use_global_device_ids=true | all-gather | bytes 786432 | tf_op jit(solution)/shard_map/all_gather | solution.py:257
  39.3 0.9 %shard_map.87 = f32[640,128]{1,0:T(8,128)S(1)} custom-call(f32[4,128,256]{2,1,0:T(8,128)S(1)} %get-tuple-element.9.spec_ref, f32[128,256]{1,0:T(8,128)S(1)} %get-tuple-element.10.own_ref, f32[2,2,128,256]{3,2,1,0:T(8,128)S(1)} %bitcast.9, f32[8,128,128]{2,1,0:T(8,128)S(1)} %copy-done), custom_call_target="tpu_custom_call" | custom-call | tf_op jit(solution)/shard_map/pallas_call | solution.py:206
  40.2 22.6 %all_to_all.11 = f32[128,1,640]{2,1,0:T(1,128)S(1)} all-to-all(f32[128,1,640]{2,1,0:T(1,128)S(1)} %bitcast.10), channel_id=1, replica_groups={{79,5,16,111,14,93,64,114,119,118,3,55,92,23,25,11,88,27,47,102,8,6,126..., dimensions={0} | all-to-all | bytes 655360 | tf_op jit(solution)/shard_map/all_to_all | solution.py:216
  62.8 0.1 shard_map.88
  62.9 0.0 copy-start.1
  62.9 0.0 copy-start.2
  62.9 0.0 copy-start.3
  63.0 7.5 %all-gather.1 = f32[512,128]{1,0:T(8,128)S(1)} all-gather(f32[128,128]{1,0:T(8,128)S(1)} %shard_map.88), channel_id=3, replica_groups=mesh['tensor'=4,'context'=128] {'tensor'}, dimensions={0}, use_global_device_ids=true | all-gather | bytes 327680 | tf_op jit(solution)/shard_map/all_gather | solution.py:263
  70.5 0.0 copy-done.1
  70.5 0.0 copy-done.2
  70.5 0.0 copy-done.3
  70.5 0.8 %shard_map.89 = (bf16[128,256]{1,0:T(8,128)(2,1)}, bf16[128,256]{1,0:T(8,128)(2,1)}, f32[128,256]{1,0:T(8,128)}) custom-call(f32[640,128]{1,0:T(8,128)S(1)} %bitcast.8, f32[4,128,128]{2,1,0:T(8,128)S(1)} %bitcast.12, bf16[128,256]{1,0:T(8,128)(2,1)S(1)} %copy-done.1, bf16[128,256]{1,0:T(8,128)(2,1)S(1)} %copy-done.2, bf16[128,256]{1,0:T(8,128)(2,1)S(1)} %copy-done.3, ...), custom_call_target="tpu_custom_call" | custom-call | tf_op jit(solution)/shard_map/pallas_call | solution.py:206
Async XLA Ops:
  0.6 34.3 %copy-start = (f32[8,128,128]{2,1,0:T(8,128)S(1)}, f32[8,128,128]{2,1,0:T(8,128)}, u32[]{:S(2)}) copy-start(f32[8,128,128]{2,1,0:T(8,128)} %constant.2.clone.table_ref) | copy-start | bytes 1572868
  62.9 7.6 %copy-start.1 = (bf16[128,256]{1,0:T(8,128)(2,1)S(1)}, bf16[128,256]{1,0:T(8,128)(2,1)}, u32[]{:S(2)}) copy-start(bf16[128,256]{1,0:T(8,128)(2,1)} %x_ref.1) | copy-start | bytes 196612
  62.9 7.6 %copy-start.2 = (bf16[128,256]{1,0:T(8,128)(2,1)S(1)}, bf16[128,256]{1,0:T(8,128)(2,1)}, u32[]{:S(2)}) copy-start(bf16[128,256]{1,0:T(8,128)(2,1)} %g_ref.1) | copy-start | bytes 196612
  62.9 7.5 %copy-start.3 = (bf16[128,256]{1,0:T(8,128)(2,1)S(1)}, bf16[128,256]{1,0:T(8,128)(2,1)}, u32[]{:S(2)}) copy-start(bf16[128,256]{1,0:T(8,128)(2,1)} %o_ref.1) | copy-start | bytes 196612

commit v4 on v3

--- a/solution.py
+++ b/solution.py
@@ -17,7 +17,7 @@
 
 
 def partners():
-    return np.random.default_rng(16).permutation(N)
+    return np.random.default_rng(52).permutation(N)
 
 
 def tables():

time: 71.5 us -> 68.8 us (0.962)
  blocking collectives: 66.7 us -> 64 us
    all_to_all x2, blocking collectives: 55.5 us -> 51.7 us  [exchange(): lax.all_to_all(field, 'context', split_axis=0, concat_axis=0, tiled=True,...]
where the time goes in v4:
time: 68.8 us; the launch traced here: 68.6 us
  blocking collectives  64 us (93%)
  Pallas kernels  3.82 us (6%)
  between operations  0.7 us (1%)
    all_to_all x2, blocking collectives, exchange(): lax.all_to_all(field, 'context', split_axis=0, concat_axis=0, tiled=True,...  51.7 us
    all_gather x1, blocking collectives, local(): share = lax.all_gather(share, 'tensor', axis=0, tiled=False)  7.91 us
    all_gather x1, blocking collectives, local(): lax.all_gather(pair, 'tensor', axis=0, tiled=False, axis_index_groups=cor...  4.39 us
    pallas_call x5, Pallas kernels, call(): pl.pallas_call(kernel, out_shape=out, compiler_params=pltpu.CompilerParam...  3.82 us

profile of v4, /device:TPU:1, one launch (start us, length us, event | category | flops | bytes accessed | tf_op | source)
XLA Modules:
  0.0 68.6 jit_solution(3321191850707912990)
XLA Ops:
  0.6 0.0 copy-start
  0.6 1.3 %shard_map.85 = (f32[640,128]{1,0:T(8,128)S(1)}, f32[1,256]{1,0:T(1,128)S(1)}) custom-call(bf16[128,256]{1,0:T(8,128)(2,1)} %x_ref.1, bf16[128,256]{1,0:T(8,128)(2,1)} %g_ref.1, f32[128,256]{1,0:T(8,128)} %f_hbm.1, bf16[128,256]{1,0:T(8,128)(2,1)} %o_ref.1, f32[1,256]{1,0:T(1,128)} %bitcast.14), custom_call_target="tpu_custom_call" | custom-call | tf_op jit(solution)/shard_map/pallas_call | solution.py:206
  1.9 29.5 %all_to_all.10 = f32[128,1,640]{2,1,0:T(1,128)S(1)} all-to-all(f32[128,1,640]{2,1,0:T(1,128)S(1)} %bitcast.13), channel_id=1, replica_groups={{118,21,62,15,46,122,124,83,99,81,92,19,17,105,8,4,6,74,57,119,27,49,70..., dimensions={0} | all-to-all | bytes 655360 | tf_op jit(solution)/shard_map/all_to_all | solution.py:216
  31.5 0.0 copy-done
  31.5 0.7 %shard_map.86 = (f32[4,128,256]{2,1,0:T(8,128)S(1)}, f32[128,256]{1,0:T(8,128)S(1)}, f32[2,128,256]{2,1,0:T(8,128)S(1)}) custom-call(f32[640,128]{1,0:T(8,128)S(1)} %bitcast.11, f32[8,128,128]{2,1,0:T(8,128)S(1)} %copy-done), custom_call_target="tpu_custom_call" | custom-call | tf_op jit(solution)/shard_map/pallas_call | solution.py:206
  32.2 4.4 %all-gather = f32[4,128,256]{2,1,0:T(8,128)S(1)} all-gather(f32[2,128,256]{2,1,0:T(8,128)S(1)} %get-tuple-element.11), channel_id=2, replica_groups={{0,128},{256,384},{1,129},{257,385},{2,130},{258,386},{3,131},{259,387}..., dimensions={0}, use_global_device_ids=true | all-gather | bytes 786432 | tf_op jit(solution)/shard_map/all_gather | solution.py:257
  36.6 0.9 %shard_map.87 = f32[640,128]{1,0:T(8,128)S(1)} custom-call(f32[4,128,256]{2,1,0:T(8,128)S(1)} %get-tuple-element.9.spec_ref, f32[128,256]{1,0:T(8,128)S(1)} %get-tuple-element.10.own_ref, f32[2,2,128,256]{3,2,1,0:T(8,128)S(1)} %bitcast.9, f32[8,128,128]{2,1,0:T(8,128)S(1)} %copy-done), custom_call_target="tpu_custom_call" | custom-call | tf_op jit(solution)/shard_map/pallas_call | solution.py:206
  37.5 22.2 %all_to_all.11 = f32[128,1,640]{2,1,0:T(1,128)S(1)} all-to-all(f32[128,1,640]{2,1,0:T(1,128)S(1)} %bitcast.10), channel_id=1, replica_groups={{118,21,62,15,46,122,124,83,99,81,92,19,17,105,8,4,6,74,57,119,27,49,70..., dimensions={0} | all-to-all | bytes 655360 | tf_op jit(solution)/shard_map/all_to_all | solution.py:216
  59.7 0.1 shard_map.88
  59.8 0.0 copy-start.1
  59.8 0.0 copy-start.2
  59.8 0.0 copy-start.3
  59.9 7.9 %all-gather.1 = f32[512,128]{1,0:T(8,128)S(1)} all-gather(f32[128,128]{1,0:T(8,128)S(1)} %shard_map.88), channel_id=3, replica_groups=mesh['tensor'=4,'context'=128] {'tensor'}, dimensions={0}, use_global_device_ids=true | all-gather | bytes 327680 | tf_op jit(solution)/shard_map/all_gather | solution.py:263
  67.8 0.0 copy-done.1
  67.8 0.0 copy-done.2
  67.8 0.0 copy-done.3
  67.8 0.8 %shard_map.89 = (bf16[128,256]{1,0:T(8,128)(2,1)}, bf16[128,256]{1,0:T(8,128)(2,1)}, f32[128,256]{1,0:T(8,128)}) custom-call(f32[640,128]{1,0:T(8,128)S(1)} %bitcast.8, f32[4,128,128]{2,1,0:T(8,128)S(1)} %bitcast.12, bf16[128,256]{1,0:T(8,128)(2,1)S(1)} %copy-done.1, bf16[128,256]{1,0:T(8,128)(2,1)S(1)} %copy-done.2, bf16[128,256]{1,0:T(8,128)(2,1)S(1)} %copy-done.3, ...), custom_call_target="tpu_custom_call" | custom-call | tf_op jit(solution)/shard_map/pallas_call | solution.py:206
Async XLA Ops:
  0.6 30.8 %copy-start = (f32[8,128,128]{2,1,0:T(8,128)S(1)}, f32[8,128,128]{2,1,0:T(8,128)}, u32[]{:S(2)}) copy-start(f32[8,128,128]{2,1,0:T(8,128)} %constant.2.clone.table_ref) | copy-start | bytes 1572868
  59.8 8.0 %copy-start.1 = (bf16[128,256]{1,0:T(8,128)(2,1)S(1)}, bf16[128,256]{1,0:T(8,128)(2,1)}, u32[]{:S(2)}) copy-start(bf16[128,256]{1,0:T(8,128)(2,1)} %x_ref.1) | copy-start | bytes 196612
  59.8 7.9 %copy-start.2 = (bf16[128,256]{1,0:T(8,128)(2,1)S(1)}, bf16[128,256]{1,0:T(8,128)(2,1)}, u32[]{:S(2)}) copy-start(bf16[128,256]{1,0:T(8,128)(2,1)} %g_ref.1) | copy-start | bytes 196612
  59.8 7.9 %copy-start.3 = (bf16[128,256]{1,0:T(8,128)(2,1)S(1)}, bf16[128,256]{1,0:T(8,128)(2,1)}, u32[]{:S(2)}) copy-start(bf16[128,256]{1,0:T(8,128)(2,1)} %o_ref.1) | copy-start | bytes 196612

commit v5 on v4

--- a/solution.py
+++ b/solution.py
@@ -16,14 +16,14 @@
 HBM = pl.BlockSpec(memory_space=pltpu.HBM)
 
 
-def partners():
-    return np.random.default_rng(52).permutation(N)
-
-
-def tables():
+def partners(side):
+    return np.random.default_rng((52, 59)[side]).permutation(N)
+
+
+def tables(side):
     length = N * N
     index = np.arange(N)
-    turn = (np.outer(4 * index + 1, partners()) % (4 * N)) * (2 * math.pi / (4 * N))
+    turn = (np.outer(4 * index + 1, partners(side)) % (4 * N)) * (2 * math.pi / (4 * N))
     first = [np.cos(turn), -np.sin(turn)]
     scale = 1.0 / (length * math.sqrt(length))
     last = [first[0].T * scale, first[1].T * scale]
@@ -132,7 +132,8 @@
 
 
 def spectra_kernel(in_ref, table_ref, spec_ref, own_ref, out_ref):
-    table = [table_ref[i] for i in range(8)]
+    side = lax.axis_index("tensor") // 2
+    table = [table_ref[side, i] for i in range(8)]
     x0, x1, m0, m1, f = forward([signal_rows(in_ref, s)[...] for s in range(S)], table)
     for s, spec in enumerate((x0, x1, m0, m1)):
         spec_ref[s] = spec
@@ -144,7 +145,8 @@
 
 
 def inverse_kernel(spec_ref, own_ref, pair_ref, table_ref, out_ref):
-    table = [table_ref[i] for i in range(8)]
+    side = lax.axis_index("tensor") // 2
+    table = [table_ref[side, i] for i in range(8)]
     f0, f1 = pair_ref[0, 0], pair_ref[1, 0]
     x0, x1, m0, m1 = (spec_ref[s] for s in range(4))
     share = own_ref[...] + pair_ref[1 - core_index(), 1]
@@ -215,11 +217,11 @@
     field = field.reshape(N, 1, S * N)
     field = lax.all_to_all(
         field,
-        "context",
+        ("tensor", "context"),
         split_axis=0,
         concat_axis=0,
         tiled=True,
-        axis_index_groups=[partners().tolist()],
+        axis_index_groups=[(t * N + partners(t // 2)).tolist() for t in range(4)],
     )
     return field.reshape(S * N, N)
 
@@ -230,7 +232,7 @@
 
 def local(inputs, gates, filters, skip, out_grad):
     tensor = lax.axis_size("tensor")
-    table = jnp.asarray(tables())
+    table = jnp.asarray(np.stack([tables(0), tables(1)]))
     sent, skip = call(
         pack_kernel,
         (pltpu.VMEM((S * N, N), F32), pltpu.VMEM((1, 2 * N), F32)),

time: 68.8 us -> 70.1 us (1.019)
  local copies, waits for them, and re-layouts: 0.03 us -> 1.25 us
    unnamed x8 -> x10, local copies, waits for them, and re-layouts: 0.03 us -> 1.25 us
where the time goes in v5:
time: 70.1 us; the launch traced here: 69.8 us
  blocking collectives  64.1 us (91%)
  Pallas kernels  3.77 us (5%)
  local copies, waits for them, and re-layouts  1.25 us (2%)
    all_to_all x2, blocking collectives, exchange(): lax.all_to_all(field, ('tensor', 'context'), split_axis=0, concat_axis=0,...  51.8 us
    all_gather x1, blocking collectives, local(): share = lax.all_gather(share, 'tensor', axis=0, tiled=False)  7.92 us
    all_gather x1, blocking collectives, local(): lax.all_gather(pair, 'tensor', axis=0, tiled=False, axis_index_groups=cor...  4.39 us
    pallas_call x5, Pallas kernels, call(): pl.pallas_call(kernel, out_shape=out, compiler_params=pltpu.CompilerParam...  3.77 us

profile of v5, /device:TPU:1, one launch (start us, length us, event | category | flops | bytes accessed | tf_op | source)
XLA Modules:
  0.0 69.8 jit_solution(13073048950413089057)
XLA Ops:
  0.6 1.2 %shard_map.85 = (f32[640,128]{1,0:T(8,128)S(1)}, f32[1,256]{1,0:T(1,128)S(1)}) custom-call(bf16[128,256]{1,0:T(8,128)(2,1)} %x_ref.1, bf16[128,256]{1,0:T(8,128)(2,1)} %g_ref.1, f32[128,256]{1,0:T(8,128)} %f_hbm.1, bf16[128,256]{1,0:T(8,128)(2,1)} %o_ref.1, f32[1,256]{1,0:T(1,128)} %bitcast.14), custom_call_target="tpu_custom_call" | custom-call | tf_op jit(solution)/shard_map/pallas_call | solution.py:208
  1.9 29.5 %all_to_all.10 = f32[128,1,640]{2,1,0:T(1,128)S(1)} all-to-all(f32[128,1,640]{2,1,0:T(1,128)S(1)} %bitcast.13), channel_id=1, replica_groups={{118,21,62,15,46,122,124,83,99,81,92,19,17,105,8,4,6,74,57,119,27,49,70..., dimensions={0} | all-to-all | bytes 655360 | tf_op jit(solution)/shard_map/all_to_all | solution.py:218
  31.4 0.0 copy-start
  31.4 1.2 %copy-done = f32[2,8,128,128]{3,2,1,0:T(8,128)S(1)} copy-done((f32[2,8,128,128]{3,2,1,0:T(8,128)S(1)}, f32[2,8,128,128]{3,2,1,0:T(8,128)}, u32[]{:S(2)}) %copy-start) | copy-done | bytes 1048600
  32.6 0.0 copy-start.1
  32.6 0.7 %shard_map.86 = (f32[4,128,256]{2,1,0:T(8,128)S(1)}, f32[128,256]{1,0:T(8,128)S(1)}, f32[2,128,256]{2,1,0:T(8,128)S(1)}) custom-call(f32[640,128]{1,0:T(8,128)S(1)} %bitcast.11, f32[2,8,128,128]{3,2,1,0:T(8,128)S(1)} %copy-done), custom_call_target="tpu_custom_call" | custom-call | tf_op jit(solution)/shard_map/pallas_call | solution.py:208
  33.4 4.4 %all-gather = f32[4,128,256]{2,1,0:T(8,128)S(1)} all-gather(f32[2,128,256]{2,1,0:T(8,128)S(1)} %get-tuple-element.11), channel_id=2, replica_groups={{0,128},{256,384},{1,129},{257,385},{2,130},{258,386},{3,131},{259,387}..., dimensions={0}, use_global_device_ids=true | all-gather | bytes 786432 | tf_op jit(solution)/shard_map/all_gather | solution.py:259
  37.8 0.0 copy-done.1
  37.8 0.9 %shard_map.87 = f32[640,128]{1,0:T(8,128)S(1)} custom-call(f32[4,128,256]{2,1,0:T(8,128)S(1)} %get-tuple-element.9.spec_ref, f32[128,256]{1,0:T(8,128)S(1)} %get-tuple-element.10.own_ref, f32[2,2,128,256]{3,2,1,0:T(8,128)S(1)} %bitcast.9, f32[2,8,128,128]{3,2,1,0:T(8,128)S(1)} %copy-done.1), custom_call_target="tpu_custom_call" | custom-call | tf_op jit(solution)/shard_map/pallas_call | solution.py:208
  38.7 22.2 %all_to_all.11 = f32[128,1,640]{2,1,0:T(1,128)S(1)} all-to-all(f32[128,1,640]{2,1,0:T(1,128)S(1)} %bitcast.10), channel_id=1, replica_groups={{118,21,62,15,46,122,124,83,99,81,92,19,17,105,8,4,6,74,57,119,27,49,70..., dimensions={0} | all-to-all | bytes 655360 | tf_op jit(solution)/shard_map/all_to_all | solution.py:218
  60.9 0.1 shard_map.88
  61.0 0.0 copy-start.2
  61.0 0.0 copy-start.3
  61.0 0.0 copy-start.4
  61.0 7.9 %all-gather.1 = f32[512,128]{1,0:T(8,128)S(1)} all-gather(f32[128,128]{1,0:T(8,128)S(1)} %shard_map.88), channel_id=3, replica_groups=mesh['tensor'=4,'context'=128] {'tensor'}, dimensions={0}, use_global_device_ids=true | all-gather | bytes 327680 | tf_op jit(solution)/shard_map/all_gather | solution.py:265
  68.9 0.0 copy-done.2
  69.0 0.0 copy-done.3
  69.0 0.0 copy-done.4
  69.0 0.8 %shard_map.89 = (bf16[128,256]{1,0:T(8,128)(2,1)}, bf16[128,256]{1,0:T(8,128)(2,1)}, f32[128,256]{1,0:T(8,128)}) custom-call(f32[640,128]{1,0:T(8,128)S(1)} %bitcast.8, f32[4,128,128]{2,1,0:T(8,128)S(1)} %bitcast.12, bf16[128,256]{1,0:T(8,128)(2,1)S(1)} %copy-done.2, bf16[128,256]{1,0:T(8,128)(2,1)S(1)} %copy-done.3, bf16[128,256]{1,0:T(8,128)(2,1)S(1)} %copy-done.4, ...), custom_call_target="tpu_custom_call" | custom-call | tf_op jit(solution)/shard_map/pallas_call | solution.py:208
Async XLA Ops:
  31.4 1.2 %copy-start = (f32[2,8,128,128]{3,2,1,0:T(8,128)S(1)}, f32[2,8,128,128]{3,2,1,0:T(8,128)}, u32[]{:S(2)}) copy-start(f32[2,8,128,128]{3,2,1,0:T(8,128)} %constant.2.clone.table_ref) | copy-start | bytes 3145732
  32.6 5.1 %copy-start.1 = (f32[2,8,128,128]{3,2,1,0:T(8,128)S(1)}, f32[2,8,128,128]{3,2,1,0:T(8,128)}, u32[]{:S(2)}) copy-start(f32[2,8,128,128]{3,2,1,0:T(8,128)} %constant.2.clone.table_ref) | copy-start | bytes 3145732
  61.0 8.0 %copy-start.2 = (bf16[128,256]{1,0:T(8,128)(2,1)S(1)}, bf16[128,256]{1,0:T(8,128)(2,1)}, u32[]{:S(2)}) copy-start(bf16[128,256]{1,0:T(8,128)(2,1)} %x_ref.1) | copy-start | bytes 196612
  61.0 7.9 %copy-start.3 = (bf16[128,256]{1,0:T(8,128)(2,1)S(1)}, bf16[128,256]{1,0:T(8,128)(2,1)}, u32[]{:S(2)}) copy-start(bf16[128,256]{1,0:T(8,128)(2,1)} %g_ref.1) | copy-start | bytes 196612
  61.0 7.9 %copy-start.4 = (bf16[128,256]{1,0:T(8,128)(2,1)S(1)}, bf16[128,256]{1,0:T(8,128)(2,1)}, u32[]{:S(2)}) copy-start(bf16[128,256]{1,0:T(8,128)(2,1)} %o_ref.1) | copy-start | bytes 196612
